TPU v7x, 32 devices: a whole 2x2x4 slice. The times are simulated.
32 devices in a mesh: stream: 8 (over y, x, core), cross: 4 (over z).
Axes of the slice: x: 2, y: 2, z: 4, core: 2. Of those that a mesh axis runs over, the one named last changes fastest.
Arguments:
- initial_state: float32 [5, 64, 32768], P(None, 'stream', 'cross'), may hold values from -6 to 6
- forcing: float32 [5, 64, 32768], P(None, 'stream', 'cross'), may hold values from -0.3 to 0.3
- block_inverse: float32 [5, 5, 64, 32768], P(None, None, 'stream', 'cross'), may hold values from -1 to 1, as said below
- lower_decay: float32 [5, 64, 32768], P(None, 'stream', 'cross'), may hold values from 0 to 1
- upper_decay: float32 [5, 64, 32768], P(None, 'stream', 'cross'), may hold values from 0 to 1
- cross_coupling: float32 [64, 32768], P('stream', 'cross'), may hold values from 0.002 to 0.02
- iblank: int32 [64, 32768], P('stream', 'cross'), may hold values 0 or 1
- donor_receiver: int32 [1024, 1], P(('stream', 'cross')), may hold values from 0 to 31; in each aligned block of 32 rows (0 to 31, 32 to 63, ...) at most 2 rows name the same one
- donor_block: int32 [1024], P(('stream', 'cross')), may hold values from 0 to 511
- stencil_offset: int32 [1024], P(('stream', 'cross')), may hold values from 1 to 127
- stencil_weight: float32 [1024, 128], P(('stream', 'cross')), may hold values from 0.005 to 0.02
- fringe_target: int32 [2048], P(('stream', 'cross')), may hold values from 0 to 511
Outputs:
- final_state: float32 [5, 64, 32768], P(None, 'stream', 'cross')
- last_update: float32 [5, 64, 32768], P(None, 'stream', 'cross')
Inputs may be any that keep to these rules, and one draw needn't show every extreme that they name: `donor_receiver`: within the rows of one device no receiving device is named more than 2 times. `block_inverse`: each 5 x 5 block is orthogonal and symmetric.
All inputs are finite; a program needn't handle non-finite values. No bound on the sum of `iblank` on one device may be relied on, other than what follows from the above.
Results may differ from a plain program's by a relative error of at most 0.00018.
Values sent between devices are 32-bit elements; how exact they have to be, the bound alone decides.
A program may use at most 128 MiB of HBM per device.

v0:
```python
import jax
import jax.numpy as jnp
from jax import lax
from jax.sharding import PartitionSpec as P

ITERS = 2
CAP = 2


def padded_2(cells, sides, width):
    for axis, dim in sides:
        count = lax.axis_size(axis)
        head = lax.slice_in_dim(cells, 0, width, axis=dim)
        tail = lax.slice_in_dim(cells, cells.shape[dim] - width, cells.shape[dim], axis=dim)
        cells = jnp.concatenate(
            [
                lax.ppermute(tail, axis, [(i, (i + 1) % count) for i in range(count)]),
                cells,
                lax.ppermute(head, axis, [((i + 1) % count, i) for i in range(count)]),
            ],
            axis=dim,
        )
    return cells


def passed_along(value, axis, steps):
    count = lax.axis_size(axis)
    initial, last = (max(0, -steps), min(count, count - steps))
    return lax.ppermute(value, axis, [(source, source + steps) for source in range(initial, last)])


def apply_block(block_inv, vector):
    return jnp.sum(block_inv * vector[None], axis=1)


def multiply_maps(left, right):
    return jnp.sum(left[:, :, None, :] * right[None], axis=1)


def plane_of(array, index, axis):
    return lax.dynamic_index_in_dim(array, index, axis, keepdims=False)


def compose_down(driving_term, block_inv, decay):
    count = driving_term.shape[1]
    cells = driving_term.shape[2]
    identity = jnp.broadcast_to(jnp.eye(5, dtype=jnp.float32)[:, :, None], (5, 5, cells))

    def step(index, carry):
        matrix, offset = carry
        inverse = plane_of(block_inv, index, 2)
        factor = plane_of(decay, index, 1)
        matrix = multiply_maps(inverse, factor[:, None, :] * matrix)
        offset = apply_block(inverse, plane_of(driving_term, index, 1) + factor * offset)
        return (matrix, offset)

    return lax.fori_loop(0, count, step, (identity, jnp.zeros((5, cells), jnp.float32)))


def compose_up(near, block_inv, decay):
    count = near.shape[1]
    cells = near.shape[2]
    identity = jnp.broadcast_to(jnp.eye(5, dtype=jnp.float32)[:, :, None], (5, 5, cells))

    def step(turn, carry):
        matrix, offset = carry
        index = count - 1 - turn
        inverse = plane_of(block_inv, index, 2)
        factor = plane_of(decay, index, 1)
        matrix = multiply_maps(inverse, factor[:, None, :] * matrix)
        offset = plane_of(near, index, 1) + apply_block(inverse, factor * offset)
        return (matrix, offset)

    return lax.fori_loop(0, count, step, (identity, jnp.zeros((5, cells), jnp.float32)))


def sweep_down(driving_term, block_inv, decay, incoming):
    count = driving_term.shape[1]

    def step(index, carry):
        face, sweep_output = carry
        face = apply_block(
            plane_of(block_inv, index, 2),
            plane_of(driving_term, index, 1) + plane_of(decay, index, 1) * face,
        )
        return (face, lax.dynamic_update_index_in_dim(sweep_output, face, index, 1))

    return lax.fori_loop(0, count, step, (incoming, jnp.zeros_like(driving_term)))[1]


def sweep_up(near, block_inv, decay, incoming):
    count = near.shape[1]

    def step(turn, carry):
        face, sweep_output = carry
        index = count - 1 - turn
        face = plane_of(near, index, 1) + apply_block(
            plane_of(block_inv, index, 2), plane_of(decay, index, 1) * face
        )
        return (face, lax.dynamic_update_index_in_dim(sweep_output, face, index, 1))

    return lax.fori_loop(0, count, step, (incoming, jnp.zeros_like(near)))[1]


def shards(
    initial_state,
    forcing,
    block_inverse,
    lower_decay,
    upper_decay,
    cross_coupling,
    iblank,
    donor_receiver,
    donor_block,
    stencil_offset,
    stencil_weight,
    fringe_target,
):
    stream_count = lax.axis_size("stream")
    cross_count = lax.axis_size("cross")
    devices = stream_count * cross_count
    planes = initial_state.shape[1]
    cells = initial_state.shape[2]
    block_count = planes * cells // 128
    senders = donor_block.shape[0]
    hole = (1 - iblank).astype(jnp.float32)
    receiver = donor_receiver[:, 0]
    order = lax.broadcasted_iota(jnp.int32, (senders, senders), 1)
    earlier = order < order.T
    same = receiver[:, None] == receiver[None, :]
    slot_rank = jnp.sum((same & earlier).astype(jnp.int32), axis=1)
    destination = receiver * CAP + slot_rank
    block_ids = lax.broadcasted_iota(jnp.int32, (senders, block_count), 1)
    pick_table = (donor_block[:, None] == block_ids).astype(jnp.float32)
    source_lane = lax.broadcasted_iota(jnp.int32, (senders, 128, 128), 1)
    target_lane = lax.broadcasted_iota(jnp.int32, (senders, 128, 128), 2)
    offset_lookup = (source_lane == (target_lane + stencil_offset[:, None, None]) % 128).astype(
        jnp.float32
    )
    slot_ids = lax.broadcasted_iota(jnp.int32, (devices * CAP, senders), 0)
    place_table = (destination[None, :] == slot_ids).astype(jnp.float32)
    column_entries = lax.broadcasted_iota(jnp.int32, (block_count, devices * CAP), 0)
    onehot = (fringe_target[None, :] == column_entries).astype(jnp.float32)
    blank_face = jnp.zeros((5, cells), jnp.float32)
    state = initial_state
    update = jnp.zeros_like(initial_state)
    for relaxation_round in range(ITERS):
        padded = padded_2(state, (("cross", 2),), 1)
        laplace = 2.0 * state - padded[:, :, :-2] - padded[:, :, 2:]
        blocks_local = state.reshape(5, block_count, 128)
        selected_values = jnp.einsum(
            "eb,vbp->vep", pick_table, blocks_local, precision=lax.Precision.HIGHEST
        )
        displaced_values = jnp.einsum(
            "mub,ubh->muh", selected_values, offset_lookup, precision=lax.Precision.HIGHEST
        )
        values = stencil_weight[None] * (selected_values + displaced_values)
        outgoing = jnp.einsum("se,vep->vsp", place_table, values, precision=lax.Precision.HIGHEST)
        received = lax.all_to_all(
            outgoing, ("stream", "cross"), split_axis=1, concat_axis=1, tiled=True
        )
        fringe = jnp.einsum(
            "bs,vsp->vbp", onehot, received, precision=lax.Precision.HIGHEST
        ).reshape(state.shape)
        driving_term = forcing - cross_coupling[None] * laplace + hole[None] * fringe
        matrix_down, offset_down = compose_down(driving_term, block_inverse, lower_decay)

        def pass_down(turn, carry):
            face, incoming = carry
            incoming = passed_along(face, "stream", 1)
            return (apply_block(matrix_down, incoming) + offset_down, incoming)

        incoming_down = lax.fori_loop(0, stream_count, pass_down, (offset_down, blank_face))[1]
        near = sweep_down(driving_term, block_inverse, lower_decay, incoming_down)
        matrix_up, offset_up = compose_up(near, block_inverse, upper_decay)

        def pass_up(turn, carry):
            face, incoming = carry
            incoming = passed_along(face, "stream", -1)
            return (apply_block(matrix_up, incoming) + offset_up, incoming)

        incoming_up = lax.fori_loop(0, stream_count, pass_up, (offset_up, blank_face))[1]
        update = sweep_up(near, block_inverse, upper_decay, incoming_up)
        state = state + update
    return (state, update)


def solution(mesh):
    return jax.shard_map(
        shards,
        mesh=mesh,
        in_specs=(
            P(None, "stream", "cross"),
            P(None, "stream", "cross"),
            P(None, None, "stream", "cross"),
            P(None, "stream", "cross"),
            P(None, "stream", "cross"),
            P("stream", "cross"),
            P("stream", "cross"),
            P(("stream", "cross"), None),
            P(("stream", "cross")),
            P(("stream", "cross")),
            P(("stream", "cross"), None),
            P(("stream", "cross")),
        ),
        out_specs=(P(None, "stream", "cross"), P(None, "stream", "cross")),
        check_vma=False,
    )
```

profile of v0, /device:TPU:3, one launch (start us, length us, event | category | flops | bytes accessed | tf_op | source)
XLA Modules:
  0.0 806.4 jit_solution(11326317212507014265)
XLA Ops:
  5.4 6.5 all-to-all-start
  15.9 11.0 %copy.72 = f32[5,5,8,8192]{3,1,0,2:T(8,128)} copy(f32[5,5,8,8192]{3,2,1,0:T(8,128)} %param.38) | data formatting | bytes 13107200
  44.0 36.2 %while.178 = (s32[]{:T(128)}, f32[5,5,8192]{2,1,0:T(8,128)S(1)}, f32[5,8192]{1,0:T(8,128)}, f32[5,5,8,8192]{3,1,0,2:T(8,128)}, f32[5,8,8192]{2,0,1:T(8,128)S(1)}, /*index=5*/f32[5,8,8192]{2,0,1:T(8,128)}, s32[]{:T(128)}) while((s32[]{:T(128)}, f32[5,5,8192]{2,1,0:T(8,128)S(1)}, f32[5,8192]{1,0:T(8,128)}, f32[5,5,8,8192]{3,1,0,2:T(8,128)}, ...), condition=%wide.region_4.5_spmd, body=%wide.region_1.4_spmd.sunk | while | flops 2498562 | bytes 7209049 | solution.py:57
  82.8 79.5 %while.179 = (s32[]{:T(128)}, f32[5,8192]{1,0:T(8,128)}, f32[5,8192]{1,0:T(8,128)}, f32[5,5,8192]{2,1,0:T(8,128)S(1)}, f32[5,8192]{1,0:T(8,128)}, /*index=5*/s32[]{:T(128)}) while((s32[]{:T(128)}, f32[5,8192]{1,0:T(8,128)}, f32[5,8192]{1,0:T(8,128)}, f32[5,5,8192]{2,1,0:T(8,128)S(1)}, f32[5,8192]{1,0:T(8,128)}, /*index=5*/s32[]{:T(128)}) %tuple.350), condition=%wide.region_7.8_spmd, body=%wide.region_5.7_spmd.sunk | while | flops 409602 | bytes 3604645 | solution.py:173
  82.8 4.0 collective-permute-start
  91.6 5.3 collective-permute-start
  101.7 5.3 collective-permute-start
  111.8 5.3 collective-permute-start
  121.9 5.3 collective-permute-start
  132.0 5.3 collective-permute-start
  142.1 5.3 collective-permute-start
  152.2 5.3 collective-permute-start
  163.3 54.0 %while.180 = (s32[]{:T(128)}, f32[5,8192]{1,0:T(8,128)S(1)}, f32[5,8,8192]{2,1,0:T(8,128)S(1)}, f32[5,5,8,8192]{3,2,1,0:T(8,128)}, f32[5,8,8192]{2,0,1:T(8,128)}...) while((s32[]{:T(128)}, f32[5,8192]{1,0:T(8,128)S(1)}, f32[5,8,8192]{2,1,0:T(8,128)S(1)}, ...), condition=%wide.region_10.11_spmd, body=%wide.region_8.10_spmd.sunk | while | flops 450562 | bytes 4096097 | solution.py:88
  164.4 3.6 constant_dynamic-slice_fusion.16
  171.1 3.6 constant_dynamic-slice_fusion.16
  177.9 3.6 constant_dynamic-slice_fusion.16
  184.6 3.6 constant_dynamic-slice_fusion.16
  198.1 3.6 constant_dynamic-slice_fusion.16
  204.9 3.6 constant_dynamic-slice_fusion.16
  211.6 3.6 constant_dynamic-slice_fusion.16
  218.2 31.9 %while.188 = (s32[]{:T(128)}, f32[5,5,8192]{2,1,0:T(8,128)S(1)}, f32[5,8192]{1,0:T(8,128)S(1)}, f32[5,5,8,8192]{3,1,0,2:T(8,128)}, f32[5,8,8192]{2,0,1:T(8,128)}...) while((s32[]{:T(128)}, f32[5,5,8192]{2,1,0:T(8,128)S(1)}, ...), condition=%wide.region_14.15_spmd.clone, body=%wide.region_11.14_spmd.clone.sunk | while | flops 2539527 | bytes 7700649 | solution.py:74
  251.5 80.3 %while.181 = (s32[]{:T(128)}, f32[5,8192]{1,0:T(8,128)}, f32[5,8192]{1,0:T(8,128)}, f32[5,5,8192]{2,1,0:T(8,128)S(1)}, f32[5,8192]{1,0:T(8,128)S(1)}, /*index=5*/s32[]{:T(128)}) while((s32[]{:T(128)}, f32[5,8192]{1,0:T(8,128)}, f32[5,8192]{1,0:T(8,128)}, f32[5,5,8192]{2,1,0:T(8,128)S(1)}, f32[5,8192]{1,0:T(8,128)S(1)}, ...), condition=%wide.region_17.18_spmd, body=%wide.region_15.17_spmd.sunk | while | flops 409602 | bytes 2949257 | solution.py:182
  253.5 7.5 collective-permute-done.1
  264.1 6.9 collective-permute-done.1
  274.0 6.9 collective-permute-done.1
  284.0 6.9 collective-permute-done.1
  293.9 6.9 collective-permute-done.1
  303.9 6.9 collective-permute-done.1
  313.8 6.9 collective-permute-done.1
  323.8 6.9 collective-permute-done.1
  333.0 82.2 %while.182 = (s32[]{:T(128)}, f32[5,8192]{1,0:T(8,128)S(1)}, f32[5,8,8192]{2,1,0:T(8,128)}, f32[5,8,8192]{2,1,0:T(8,128)S(1)}, f32[5,5,8,8192]{3,2,1,0:T(8,128)}...) while((s32[]{:T(128)}, f32[5,8192]{1,0:T(8,128)S(1)}, ...), condition=%wide.region_20.21_spmd, body=%wide.region_18.20_spmd.sunk | while | flops 491526 | bytes 4751523 | solution.py:102
  333.0 3.7 constant_dynamic-slice_fusion.17
  339.0 4.2 dynamic_update_slice.41
  349.3 4.2 dynamic_update_slice.41
  359.5 4.2 dynamic_update_slice.41
  369.8 4.2 dynamic_update_slice.41
  380.0 4.2 dynamic_update_slice.41
  390.3 4.2 dynamic_update_slice.41
  400.6 4.2 dynamic_update_slice.41
  410.8 4.2 dynamic_update_slice.41
  426.0 6.9 all-to-all-done.1
  441.1 38.1 %while.183 = (s32[]{:T(128)}, f32[5,5,8192]{2,1,0:T(8,128)S(1)}, f32[5,8192]{1,0:T(8,128)S(1)}, f32[5,5,8,8192]{3,1,0,2:T(8,128)}, f32[5,8,8192]{2,0,1:T(8,128)}, /*index=5*/f32[5,8,8192]{2,0,1:T(8,128)}, s32[]{:T(128)}) while((s32[]{:T(128)}, f32[5,5,8192]{2,1,0:T(8,128)S(1)}, f32[5,8192]{1,0:T(8,128)S(1)}, f32[5,5,8,8192]{3,1,0,2:T(8,128)}, ...), condition=%wide.region_24.25_spmd, body=%wide.region_21.24_spmd.sunk | while | flops 2498562 | bytes 7209049 | solution.py:57
  480.6 77.4 %while.184 = (s32[]{:T(128)}, f32[5,8192]{1,0:T(8,128)}, f32[5,8192]{1,0:T(8,128)}, f32[5,5,8192]{2,1,0:T(8,128)S(1)}, f32[5,8192]{1,0:T(8,128)S(1)}, /*index=5*/s32[]{:T(128)}) while((s32[]{:T(128)}, f32[5,8192]{1,0:T(8,128)}, f32[5,8192]{1,0:T(8,128)}, f32[5,5,8192]{2,1,0:T(8,128)S(1)}, f32[5,8192]{1,0:T(8,128)S(1)}, ...), condition=%wide.region_27.28_spmd, body=%wide.region_25.27_spmd.sunk | while | flops 409602 | bytes 2949257 | solution.py:173
  488.3 5.2 collective-permute-start.2
  498.3 5.2 collective-permute-start.2
  508.2 5.2 collective-permute-start.2
  518.2 5.2 collective-permute-start.2
  528.1 5.2 collective-permute-start.2
  538.1 5.2 collective-permute-start.2
  548.1 5.2 collective-permute-start.2
  559.0 54.0 %while.185 = (s32[]{:T(128)}, f32[5,8192]{1,0:T(8,128)S(1)}, f32[5,8,8192]{2,1,0:T(8,128)S(1)}, f32[5,5,8,8192]{3,2,1,0:T(8,128)}, f32[5,8,8192]{2,0,1:T(8,128)}...) while((s32[]{:T(128)}, f32[5,8192]{1,0:T(8,128)S(1)}, f32[5,8,8192]{2,1,0:T(8,128)S(1)}, ...), condition=%wide.region_30.31_spmd, body=%wide.region_28.30_spmd.sunk | while | flops 450562 | bytes 4096097 | solution.py:88
  560.0 3.6 constant_dynamic-slice_fusion.18
  566.8 3.6 constant_dynamic-slice_fusion.18
  614.2 42.2 %while.189 = (s32[]{:T(128)}, f32[5,5,8192]{2,1,0:T(8,128)S(1)}, f32[5,8192]{1,0:T(8,128)S(1)}, f32[5,5,8,8192]{3,1,0,2:T(8,128)}, f32[5,8,8192]{2,0,1:T(8,128)}...) while((s32[]{:T(128)}, f32[5,5,8192]{2,1,0:T(8,128)S(1)}, ...), condition=%wide.region_34.35_spmd.clone, body=%wide.region_31.34_spmd.clone.sunk | while | flops 2539527 | bytes 7700649 | solution.py:74
  657.8 80.3 %while.186 = (s32[]{:T(128)}, f32[5,8192]{1,0:T(8,128)}, f32[5,8192]{1,0:T(8,128)}, f32[5,5,8192]{2,1,0:T(8,128)S(1)}, f32[5,8192]{1,0:T(8,128)S(1)}, /*index=5*/s32[]{:T(128)}) while((s32[]{:T(128)}, f32[5,8192]{1,0:T(8,128)}, f32[5,8192]{1,0:T(8,128)}, f32[5,5,8192]{2,1,0:T(8,128)S(1)}, f32[5,8192]{1,0:T(8,128)S(1)}, ...), condition=%wide.region_37.38_spmd, body=%wide.region_35.37_spmd.sunk | while | flops 409602 | bytes 2949257 | solution.py:182
  659.7 7.5 collective-permute-done.3
  670.3 6.9 collective-permute-done.3
  680.3 6.9 collective-permute-done.3
  690.2 6.9 collective-permute-done.3
  700.2 6.9 collective-permute-done.3
  710.1 6.9 collective-permute-done.3
  720.1 6.9 collective-permute-done.3
  730.0 6.9 collective-permute-done.3
  739.0 65.9 %while.187 = (s32[]{:T(128)}, f32[5,8192]{1,0:T(8,128)S(1)}, f32[5,8,8192]{2,1,0:T(8,128)S(1)}, f32[5,8,8192]{2,1,0:T(8,128)}, f32[5,5,8,8192]{3,2,1,0:T(8,128)}...) while((s32[]{:T(128)}, f32[5,8192]{1,0:T(8,128)S(1)}, ...), condition=%wide.region_40.41_spmd, body=%wide.region_38.40_spmd.sunk | while | flops 491526 | bytes 4751523 | solution.py:102
  (579 shorter events, 519.0 us)
Async XLA Ops:
  0.6 1.5 copy-start.23
  0.6 1.7 copy-start.21
  3.0 1.2 copy-start.20
  3.0 8.9 %copy-start.11 = (f32[5,8,8192]{2,1,0:T(8,128)S(1)}, f32[5,8,8192]{2,1,0:T(8,128)}, u32[]{:S(2)}) copy-start(f32[5,8,8192]{2,1,0:T(8,128)} %param.36) | copy-start | bytes 3932164
  4.2 11.0 %copy-start.19 = (s32[8,8192]{1,0:T(8,128)S(1)}, s32[8,8192]{1,0:T(8,128)}, u32[]{:S(2)}) copy-start(s32[8,8192]{1,0:T(8,128)} %param.42) | copy-start | bytes 786436
  5.4 25.0 %all-to-all-start = ((f32[5,64,128]{2,0,1:T(8,128)}), f32[5,64,128]{2,0,1:T(8,128)}, u32[]{:S(2)}, u32[]{:S(2)}) async-start(f32[5,64,128]{2,0,1:T(8,128)} %copy.64), calls=%async_computation | async-start | bytes 524288 | tf_op jit(solution)/shard_map/all_to_all | solution.py:159
  11.9 26.4 %collective-permute-start.4 = (f32[5,8,1]{2,1,0:T(8,128)S(1)}, f32[5,8,1]{2,1,0:T(8,128)S(1)}, u32[]{:S(2)}, u32[]{:S(2)}) collective-permute-start(f32[5,8,1]{2,1,0:T(8,128)S(1)} %get-tuple-element.1570), channel_id=1, source_target_pairs={{0,1},{1,2},{2,3},{3,0},{4,5},{5,6},{6,7},{7,4},{8,9},{9,10},{10,1... | collective-permute-start | bytes 488 | tf_op jit(solution)/shard_map/ppermute | solution.py:17
  13.1 25.3 %collective-permute-start.5 = (f32[5,8,1]{2,1,0:T(8,128)S(1)}, f32[5,8,1]{2,1,0:T(8,128)S(1)}, u32[]{:S(2)}, u32[]{:S(2)}) collective-permute-start(f32[5,8,1]{2,1,0:T(8,128)S(1)} %get-tuple-element.1571), channel_id=1, source_target_pairs={{1,0},{2,1},{3,2},{0,3},{5,4},{6,5},{7,6},{4,7},{9,8},{10,9},{11,1... | collective-permute-start | bytes 488 | tf_op jit(solution)/shard_map/ppermute | solution.py:19
  15.9 11.0 %copy-start.16 = (f32[5,8,8192]{2,1,0:T(8,128)S(1)}, f32[5,8,8192]{2,1,0:T(8,128)}, u32[]{:S(2)}) copy-start(f32[5,8,8192]{2,1,0:T(8,128)} %param.39) | copy-start | bytes 3932164
  26.9 1.3 copy-start.17
  28.2 2.1 copy-start.22
  80.2 2.6 copy-start.4
  82.8 8.1 %copy-start.5 = (f32[5,8192]{1,0:T(8,128)S(1)}, f32[5,8192]{1,0:T(8,128)}, u32[]{:S(2)}) copy-start(f32[5,8192]{1,0:T(8,128)} %get-tuple-element.2061) | copy-start | bytes 491524 | tf_op jit(solution)/shard_map/while
  82.8 7.6 collective-permute-start
  90.5 1.2 copy-start
  91.6 9.4 %copy-start.5 = (f32[5,8192]{1,0:T(8,128)S(1)}, f32[5,8192]{1,0:T(8,128)}, u32[]{:S(2)}) copy-start(f32[5,8192]{1,0:T(8,128)} %get-tuple-element.2061) | copy-start | bytes 491524 | tf_op jit(solution)/shard_map/while
  91.6 8.9 %collective-permute-start = (f32[5,8192]{1,0:T(8,128)}, f32[5,8192]{1,0:T(8,128)S(1)}, u32[]{:S(2)}, u32[]{:S(2)}) collective-permute-start(f32[5,8192]{1,0:T(8,128)} %get-tuple-element.2052), channel_id=1, source_target_pairs={{0,4},{4,8},{8,12},{12,16},{16,20},{20,24},{24,28},{1,5},{5,9},{9,... | collective-permute-start | bytes 491528 | tf_op jit(solution)/shard_map/while/body/eval_jaxpr/ppermute | solution.py:29
  100.6 1.2 copy-start
  101.7 9.4 %copy-start.5 = (f32[5,8192]{1,0:T(8,128)S(1)}, f32[5,8192]{1,0:T(8,128)}, u32[]{:S(2)}) copy-start(f32[5,8192]{1,0:T(8,128)} %get-tuple-element.2061) | copy-start | bytes 491524 | tf_op jit(solution)/shard_map/while
  101.7 8.9 %collective-permute-start = (f32[5,8192]{1,0:T(8,128)}, f32[5,8192]{1,0:T(8,128)S(1)}, u32[]{:S(2)}, u32[]{:S(2)}) collective-permute-start(f32[5,8192]{1,0:T(8,128)} %get-tuple-element.2052), channel_id=1, source_target_pairs={{0,4},{4,8},{8,12},{12,16},{16,20},{20,24},{24,28},{1,5},{5,9},{9,... | collective-permute-start | bytes 491528 | tf_op jit(solution)/shard_map/while/body/eval_jaxpr/ppermute | solution.py:29
  110.7 1.2 copy-start
  111.8 9.4 %copy-start.5 = (f32[5,8192]{1,0:T(8,128)S(1)}, f32[5,8192]{1,0:T(8,128)}, u32[]{:S(2)}) copy-start(f32[5,8192]{1,0:T(8,128)} %get-tuple-element.2061) | copy-start | bytes 491524 | tf_op jit(solution)/shard_map/while
  111.8 8.9 %collective-permute-start = (f32[5,8192]{1,0:T(8,128)}, f32[5,8192]{1,0:T(8,128)S(1)}, u32[]{:S(2)}, u32[]{:S(2)}) collective-permute-start(f32[5,8192]{1,0:T(8,128)} %get-tuple-element.2052), channel_id=1, source_target_pairs={{0,4},{4,8},{8,12},{12,16},{16,20},{20,24},{24,28},{1,5},{5,9},{9,... | collective-permute-start | bytes 491528 | tf_op jit(solution)/shard_map/while/body/eval_jaxpr/ppermute | solution.py:29
  120.8 1.2 copy-start
  121.9 9.4 %copy-start.5 = (f32[5,8192]{1,0:T(8,128)S(1)}, f32[5,8192]{1,0:T(8,128)}, u32[]{:S(2)}) copy-start(f32[5,8192]{1,0:T(8,128)} %get-tuple-element.2061) | copy-start | bytes 491524 | tf_op jit(solution)/shard_map/while
  121.9 8.9 %collective-permute-start = (f32[5,8192]{1,0:T(8,128)}, f32[5,8192]{1,0:T(8,128)S(1)}, u32[]{:S(2)}, u32[]{:S(2)}) collective-permute-start(f32[5,8192]{1,0:T(8,128)} %get-tuple-element.2052), channel_id=1, source_target_pairs={{0,4},{4,8},{8,12},{12,16},{16,20},{20,24},{24,28},{1,5},{5,9},{9,... | collective-permute-start | bytes 491528 | tf_op jit(solution)/shard_map/while/body/eval_jaxpr/ppermute | solution.py:29
  130.9 1.2 copy-start
  132.0 9.4 %copy-start.5 = (f32[5,8192]{1,0:T(8,128)S(1)}, f32[5,8192]{1,0:T(8,128)}, u32[]{:S(2)}) copy-start(f32[5,8192]{1,0:T(8,128)} %get-tuple-element.2061) | copy-start | bytes 491524 | tf_op jit(solution)/shard_map/while
  132.0 8.9 %collective-permute-start = (f32[5,8192]{1,0:T(8,128)}, f32[5,8192]{1,0:T(8,128)S(1)}, u32[]{:S(2)}, u32[]{:S(2)}) collective-permute-start(f32[5,8192]{1,0:T(8,128)} %get-tuple-element.2052), channel_id=1, source_target_pairs={{0,4},{4,8},{8,12},{12,16},{16,20},{20,24},{24,28},{1,5},{5,9},{9,... | collective-permute-start | bytes 491528 | tf_op jit(solution)/shard_map/while/body/eval_jaxpr/ppermute | solution.py:29
  142.1 9.4 %copy-start.5 = (f32[5,8192]{1,0:T(8,128)S(1)}, f32[5,8192]{1,0:T(8,128)}, u32[]{:S(2)}) copy-start(f32[5,8192]{1,0:T(8,128)} %get-tuple-element.2061) | copy-start | bytes 491524 | tf_op jit(solution)/shard_map/while
  142.1 8.9 %collective-permute-start = (f32[5,8192]{1,0:T(8,128)}, f32[5,8192]{1,0:T(8,128)S(1)}, u32[]{:S(2)}, u32[]{:S(2)}) collective-permute-start(f32[5,8192]{1,0:T(8,128)} %get-tuple-element.2052), channel_id=1, source_target_pairs={{0,4},{4,8},{8,12},{12,16},{16,20},{20,24},{24,28},{1,5},{5,9},{9,... | collective-permute-start | bytes 491528 | tf_op jit(solution)/shard_map/while/body/eval_jaxpr/ppermute | solution.py:29
  152.2 9.4 %copy-start.5 = (f32[5,8192]{1,0:T(8,128)S(1)}, f32[5,8192]{1,0:T(8,128)}, u32[]{:S(2)}) copy-start(f32[5,8192]{1,0:T(8,128)} %get-tuple-element.2061) | copy-start | bytes 491524 | tf_op jit(solution)/shard_map/while
  152.2 8.9 %collective-permute-start = (f32[5,8192]{1,0:T(8,128)}, f32[5,8192]{1,0:T(8,128)S(1)}, u32[]{:S(2)}, u32[]{:S(2)}) collective-permute-start(f32[5,8192]{1,0:T(8,128)} %get-tuple-element.2052), channel_id=1, source_target_pairs={{0,4},{4,8},{8,12},{12,16},{16,20},{20,24},{24,28},{1,5},{5,9},{9,... | collective-permute-start | bytes 491528 | tf_op jit(solution)/shard_map/while/body/eval_jaxpr/ppermute | solution.py:29
  251.5 9.4 %collective-permute-start.1 = (f32[5,8192]{1,0:T(8,128)}, f32[5,8192]{1,0:T(8,128)S(1)}, u32[]{:S(2)}, u32[]{:S(2)}) collective-permute-start(f32[5,8192]{1,0:T(8,128)} %get-tuple-element.2124), channel_id=1, source_target_pairs={{4,0},{8,4},{12,8},{16,12},{20,16},{24,20},{28,24},{5,1},{9,5},{13... | collective-permute-start | bytes 491528 | tf_op jit(solution)/shard_map/while/body/eval_jaxpr/ppermute | solution.py:29
  262.1 8.8 %collective-permute-start.1 = (f32[5,8192]{1,0:T(8,128)}, f32[5,8192]{1,0:T(8,128)S(1)}, u32[]{:S(2)}, u32[]{:S(2)}) collective-permute-start(f32[5,8192]{1,0:T(8,128)} %get-tuple-element.2124), channel_id=1, source_target_pairs={{4,0},{8,4},{12,8},{16,12},{20,16},{24,20},{28,24},{5,1},{9,5},{13... | collective-permute-start | bytes 491528 | tf_op jit(solution)/shard_map/while/body/eval_jaxpr/ppermute | solution.py:29
  272.1 8.8 %collective-permute-start.1 = (f32[5,8192]{1,0:T(8,128)}, f32[5,8192]{1,0:T(8,128)S(1)}, u32[]{:S(2)}, u32[]{:S(2)}) collective-permute-start(f32[5,8192]{1,0:T(8,128)} %get-tuple-element.2124), channel_id=1, source_target_pairs={{4,0},{8,4},{12,8},{16,12},{20,16},{24,20},{28,24},{5,1},{9,5},{13... | collective-permute-start | bytes 491528 | tf_op jit(solution)/shard_map/while/body/eval_jaxpr/ppermute | solution.py:29
  282.1 8.8 %collective-permute-start.1 = (f32[5,8192]{1,0:T(8,128)}, f32[5,8192]{1,0:T(8,128)S(1)}, u32[]{:S(2)}, u32[]{:S(2)}) collective-permute-start(f32[5,8192]{1,0:T(8,128)} %get-tuple-element.2124), channel_id=1, source_target_pairs={{4,0},{8,4},{12,8},{16,12},{20,16},{24,20},{28,24},{5,1},{9,5},{13... | collective-permute-start | bytes 491528 | tf_op jit(solution)/shard_map/while/body/eval_jaxpr/ppermute | solution.py:29
  292.0 8.8 %collective-permute-start.1 = (f32[5,8192]{1,0:T(8,128)}, f32[5,8192]{1,0:T(8,128)S(1)}, u32[]{:S(2)}, u32[]{:S(2)}) collective-permute-start(f32[5,8192]{1,0:T(8,128)} %get-tuple-element.2124), channel_id=1, source_target_pairs={{4,0},{8,4},{12,8},{16,12},{20,16},{24,20},{28,24},{5,1},{9,5},{13... | collective-permute-start | bytes 491528 | tf_op jit(solution)/shard_map/while/body/eval_jaxpr/ppermute | solution.py:29
  302.0 8.8 %collective-permute-start.1 = (f32[5,8192]{1,0:T(8,128)}, f32[5,8192]{1,0:T(8,128)S(1)}, u32[]{:S(2)}, u32[]{:S(2)}) collective-permute-start(f32[5,8192]{1,0:T(8,128)} %get-tuple-element.2124), channel_id=1, source_target_pairs={{4,0},{8,4},{12,8},{16,12},{20,16},{24,20},{28,24},{5,1},{9,5},{13... | collective-permute-start | bytes 491528 | tf_op jit(solution)/shard_map/while/body/eval_jaxpr/ppermute | solution.py:29
  311.9 8.8 %collective-permute-start.1 = (f32[5,8192]{1,0:T(8,128)}, f32[5,8192]{1,0:T(8,128)S(1)}, u32[]{:S(2)}, u32[]{:S(2)}) collective-permute-start(f32[5,8192]{1,0:T(8,128)} %get-tuple-element.2124), channel_id=1, source_target_pairs={{4,0},{8,4},{12,8},{16,12},{20,16},{24,20},{28,24},{5,1},{9,5},{13... | collective-permute-start | bytes 491528 | tf_op jit(solution)/shard_map/while/body/eval_jaxpr/ppermute | solution.py:29
  321.9 8.8 %collective-permute-start.1 = (f32[5,8192]{1,0:T(8,128)}, f32[5,8192]{1,0:T(8,128)S(1)}, u32[]{:S(2)}, u32[]{:S(2)}) collective-permute-start(f32[5,8192]{1,0:T(8,128)} %get-tuple-element.2124), channel_id=1, source_target_pairs={{4,0},{8,4},{12,8},{16,12},{20,16},{24,20},{28,24},{5,1},{9,5},{13... | collective-permute-start | bytes 491528 | tf_op jit(solution)/shard_map/while/body/eval_jaxpr/ppermute | solution.py:29
  333.0 82.2 %copy-start.12 = (f32[5,8,8192]{2,1,0:T(8,128)S(1)}, f32[5,8,8192]{2,1,0:T(8,128)}, u32[]{:S(2)}) copy-start(f32[5,8,8192]{2,1,0:T(8,128)} %param.36) | copy-start | bytes 3932164
  419.8 13.1 %all-to-all-start.1 = ((f32[5,64,128]{2,0,1:T(8,128)}), f32[5,64,128]{2,0,1:T(8,128)S(1)}, u32[]{:S(2)}, u32[]{:S(2)}) async-start(f32[5,64,128]{2,0,1:T(8,128)} %copy.77), calls=%async_computation.1 | async-start | bytes 524288 | tf_op jit(solution)/shard_map/all_to_all | solution.py:159
  422.7 13.9 %collective-permute-start.6 = (f32[5,8,1]{2,1,0:T(8,128)S(1)}, f32[5,8,1]{2,1,0:T(8,128)S(1)}, u32[]{:S(2)}, u32[]{:S(2)}) collective-permute-start(f32[5,8,1]{2,1,0:T(8,128)S(1)} %get-tuple-element.1568), channel_id=1, source_target_pairs={{0,1},{1,2},{2,3},{3,0},{4,5},{5,6},{6,7},{7,4},{8,9},{9,10},{10,1... | collective-permute-start | bytes 488 | tf_op jit(solution)/shard_map/ppermute | solution.py:17
  423.9 12.8 %collective-permute-start.7 = (f32[5,8,1]{2,1,0:T(8,128)S(1)}, f32[5,8,1]{2,1,0:T(8,128)S(1)}, u32[]{:S(2)}, u32[]{:S(2)}) collective-permute-start(f32[5,8,1]{2,1,0:T(8,128)S(1)} %get-tuple-element.1569), channel_id=1, source_target_pairs={{1,0},{2,1},{3,2},{0,3},{5,4},{6,5},{7,6},{4,7},{9,8},{10,9},{11,1... | collective-permute-start | bytes 488 | tf_op jit(solution)/shard_map/ppermute | solution.py:19
  435.1 1.6 copy-start.15
  435.1 1.6 copy-start.18
  480.6 6.6 collective-permute-start.2
  488.3 8.8 %collective-permute-start.2 = (f32[5,8192]{1,0:T(8,128)}, f32[5,8192]{1,0:T(8,128)S(1)}, u32[]{:S(2)}, u32[]{:S(2)}) collective-permute-start(f32[5,8192]{1,0:T(8,128)} %get-tuple-element.2193), channel_id=1, source_target_pairs={{0,4},{4,8},{8,12},{12,16},{16,20},{20,24},{24,28},{1,5},{5,9},{9,... | collective-permute-start | bytes 491528 | tf_op jit(solution)/shard_map/while/body/eval_jaxpr/ppermute | solution.py:29
  498.3 8.8 %collective-permute-start.2 = (f32[5,8192]{1,0:T(8,128)}, f32[5,8192]{1,0:T(8,128)S(1)}, u32[]{:S(2)}, u32[]{:S(2)}) collective-permute-start(f32[5,8192]{1,0:T(8,128)} %get-tuple-element.2193), channel_id=1, source_target_pairs={{0,4},{4,8},{8,12},{12,16},{16,20},{20,24},{24,28},{1,5},{5,9},{9,... | collective-permute-start | bytes 491528 | tf_op jit(solution)/shard_map/while/body/eval_jaxpr/ppermute | solution.py:29
  508.2 8.8 %collective-permute-start.2 = (f32[5,8192]{1,0:T(8,128)}, f32[5,8192]{1,0:T(8,128)S(1)}, u32[]{:S(2)}, u32[]{:S(2)}) collective-permute-start(f32[5,8192]{1,0:T(8,128)} %get-tuple-element.2193), channel_id=1, source_target_pairs={{0,4},{4,8},{8,12},{12,16},{16,20},{20,24},{24,28},{1,5},{5,9},{9,... | collective-permute-start | bytes 491528 | tf_op jit(solution)/shard_map/while/body/eval_jaxpr/ppermute | solution.py:29
  518.2 8.8 %collective-permute-start.2 = (f32[5,8192]{1,0:T(8,128)}, f32[5,8192]{1,0:T(8,128)S(1)}, u32[]{:S(2)}, u32[]{:S(2)}) collective-permute-start(f32[5,8192]{1,0:T(8,128)} %get-tuple-element.2193), channel_id=1, source_target_pairs={{0,4},{4,8},{8,12},{12,16},{16,20},{20,24},{24,28},{1,5},{5,9},{9,... | collective-permute-start | bytes 491528 | tf_op jit(solution)/shard_map/while/body/eval_jaxpr/ppermute | solution.py:29
  528.1 8.8 %collective-permute-start.2 = (f32[5,8192]{1,0:T(8,128)}, f32[5,8192]{1,0:T(8,128)S(1)}, u32[]{:S(2)}, u32[]{:S(2)}) collective-permute-start(f32[5,8192]{1,0:T(8,128)} %get-tuple-element.2193), channel_id=1, source_target_pairs={{0,4},{4,8},{8,12},{12,16},{16,20},{20,24},{24,28},{1,5},{5,9},{9,... | collective-permute-start | bytes 491528 | tf_op jit(solution)/shard_map/while/body/eval_jaxpr/ppermute | solution.py:29
  538.1 8.8 %collective-permute-start.2 = (f32[5,8192]{1,0:T(8,128)}, f32[5,8192]{1,0:T(8,128)S(1)}, u32[]{:S(2)}, u32[]{:S(2)}) collective-permute-start(f32[5,8192]{1,0:T(8,128)} %get-tuple-element.2193), channel_id=1, source_target_pairs={{0,4},{4,8},{8,12},{12,16},{16,20},{20,24},{24,28},{1,5},{5,9},{9,... | collective-permute-start | bytes 491528 | tf_op jit(solution)/shard_map/while/body/eval_jaxpr/ppermute | solution.py:29
  548.1 8.8 %collective-permute-start.2 = (f32[5,8192]{1,0:T(8,128)}, f32[5,8192]{1,0:T(8,128)S(1)}, u32[]{:S(2)}, u32[]{:S(2)}) collective-permute-start(f32[5,8192]{1,0:T(8,128)} %get-tuple-element.2193), channel_id=1, source_target_pairs={{0,4},{4,8},{8,12},{12,16},{16,20},{20,24},{24,28},{1,5},{5,9},{9,... | collective-permute-start | bytes 491528 | tf_op jit(solution)/shard_map/while/body/eval_jaxpr/ppermute | solution.py:29
  657.8 9.4 %collective-permute-start.3 = (f32[5,8192]{1,0:T(8,128)}, f32[5,8192]{1,0:T(8,128)S(1)}, u32[]{:S(2)}, u32[]{:S(2)}) collective-permute-start(f32[5,8192]{1,0:T(8,128)} %get-tuple-element.2265), channel_id=1, source_target_pairs={{4,0},{8,4},{12,8},{16,12},{20,16},{24,20},{28,24},{5,1},{9,5},{13... | collective-permute-start | bytes 491528 | tf_op jit(solution)/shard_map/while/body/eval_jaxpr/ppermute | solution.py:29
  668.4 8.8 %collective-permute-start.3 = (f32[5,8192]{1,0:T(8,128)}, f32[5,8192]{1,0:T(8,128)S(1)}, u32[]{:S(2)}, u32[]{:S(2)}) collective-permute-start(f32[5,8192]{1,0:T(8,128)} %get-tuple-element.2265), channel_id=1, source_target_pairs={{4,0},{8,4},{12,8},{16,12},{20,16},{24,20},{28,24},{5,1},{9,5},{13... | collective-permute-start | bytes 491528 | tf_op jit(solution)/shard_map/while/body/eval_jaxpr/ppermute | solution.py:29
  678.3 8.8 %collective-permute-start.3 = (f32[5,8192]{1,0:T(8,128)}, f32[5,8192]{1,0:T(8,128)S(1)}, u32[]{:S(2)}, u32[]{:S(2)}) collective-permute-start(f32[5,8192]{1,0:T(8,128)} %get-tuple-element.2265), channel_id=1, source_target_pairs={{4,0},{8,4},{12,8},{16,12},{20,16},{24,20},{28,24},{5,1},{9,5},{13... | collective-permute-start | bytes 491528 | tf_op jit(solution)/shard_map/while/body/eval_jaxpr/ppermute | solution.py:29
  688.3 8.8 %collective-permute-start.3 = (f32[5,8192]{1,0:T(8,128)}, f32[5,8192]{1,0:T(8,128)S(1)}, u32[]{:S(2)}, u32[]{:S(2)}) collective-permute-start(f32[5,8192]{1,0:T(8,128)} %get-tuple-element.2265), channel_id=1, source_target_pairs={{4,0},{8,4},{12,8},{16,12},{20,16},{24,20},{28,24},{5,1},{9,5},{13... | collective-permute-start | bytes 491528 | tf_op jit(solution)/shard_map/while/body/eval_jaxpr/ppermute | solution.py:29
  698.3 8.8 %collective-permute-start.3 = (f32[5,8192]{1,0:T(8,128)}, f32[5,8192]{1,0:T(8,128)S(1)}, u32[]{:S(2)}, u32[]{:S(2)}) collective-permute-start(f32[5,8192]{1,0:T(8,128)} %get-tuple-element.2265), channel_id=1, source_target_pairs={{4,0},{8,4},{12,8},{16,12},{20,16},{24,20},{28,24},{5,1},{9,5},{13... | collective-permute-start | bytes 491528 | tf_op jit(solution)/shard_map/while/body/eval_jaxpr/ppermute | solution.py:29
  708.2 8.8 %collective-permute-start.3 = (f32[5,8192]{1,0:T(8,128)}, f32[5,8192]{1,0:T(8,128)S(1)}, u32[]{:S(2)}, u32[]{:S(2)}) collective-permute-start(f32[5,8192]{1,0:T(8,128)} %get-tuple-element.2265), channel_id=1, source_target_pairs={{4,0},{8,4},{12,8},{16,12},{20,16},{24,20},{28,24},{5,1},{9,5},{13... | collective-permute-start | bytes 491528 | tf_op jit(solution)/shard_map/while/body/eval_jaxpr/ppermute | solution.py:29
  718.2 8.8 %collective-permute-start.3 = (f32[5,8192]{1,0:T(8,128)}, f32[5,8192]{1,0:T(8,128)S(1)}, u32[]{:S(2)}, u32[]{:S(2)}) collective-permute-start(f32[5,8192]{1,0:T(8,128)} %get-tuple-element.2265), channel_id=1, source_target_pairs={{4,0},{8,4},{12,8},{16,12},{20,16},{24,20},{28,24},{5,1},{9,5},{13... | collective-permute-start | bytes 491528 | tf_op jit(solution)/shard_map/while/body/eval_jaxpr/ppermute | solution.py:29
  728.1 8.8 %collective-permute-start.3 = (f32[5,8192]{1,0:T(8,128)}, f32[5,8192]{1,0:T(8,128)S(1)}, u32[]{:S(2)}, u32[]{:S(2)}) collective-permute-start(f32[5,8192]{1,0:T(8,128)} %get-tuple-element.2265), channel_id=1, source_target_pairs={{4,0},{8,4},{12,8},{16,12},{20,16},{24,20},{28,24},{5,1},{9,5},{13... | collective-permute-start | bytes 491528 | tf_op jit(solution)/shard_map/while/body/eval_jaxpr/ppermute | solution.py:29
  804.9 1.5 copy-start.14
  (34 other events, 38.4 us)
where the time goes:
time: 813 us; the launch traced here: 806 us
  other arithmetic  254 us (31%)
  local copies, waits for them, and re-layouts  238 us (29%)
  waiting for transfers between devices  176 us (22%)
  starting transfers between devices  127 us (16%)
    ppermute x32, waiting for transfers between devices, passed_along(): lax.ppermute(value, axis, [(source, source + steps) for source in range(i...  169 us
    dynamic_slice x48, local copies, waits for them, and re-layouts, plane_of(): return lax.dynamic_index_in_dim(array, index, axis, keepdims=False)  129 us
    reduce_sum x96, other arithmetic, apply_block(): return jnp.sum(block_inv * vector[None], axis=1)  116 us
    ppermute x32, starting transfers between devices, passed_along(): lax.ppermute(value, axis, [(source, source + steps) for source in range(i...  111 us
    dynamic_update_slice x32, local copies, waits for them, and re-layouts, step(): return (face, lax.dynamic_update_index_in_dim(sweep_output, face, index, 1))  54.3 us
    unnamed x46, local copies, waits for them, and re-layouts  22.3 us
    reduce_sum x32, other arithmetic, multiply_maps(): return jnp.sum(left[:, :, None, :] * right[None], axis=1)  21.3 us
    add x16, other arithmetic, step(): plane_of(driving_term, index, 1) + plane_of(decay, index, 1) * face  17.3 us
  transfers between devices with their start and end apart: 38, of which 33 were waited for; matrix products, arithmetic and copies ran while one was open for 3% of the time, Pallas kernels for 0%

commit v1 on v0

--- a/solution.py
+++ b/solution.py
@@ -156,8 +156,14 @@
         )
         values = stencil_weight[None] * (selected_values + displaced_values)
         outgoing = jnp.einsum("se,vep->vsp", place_table, values, precision=lax.Precision.HIGHEST)
-        received = lax.all_to_all(
-            outgoing, ("stream", "cross"), split_axis=1, concat_axis=1, tiled=True
+        received = jnp.concatenate(
+            lax.all_to_all(
+                jnp.stack(jnp.split(outgoing, lax.axis_size(("stream", "cross")), axis=1)),
+                ("stream", "cross"),
+                0,
+                0,
+            ),
+            axis=1,
         )
         fringe = jnp.einsum(
             "bs,vsp->vbp", onehot, received, precision=lax.Precision.HIGHEST

time: 813 us -> 848 us (1.043)
  local copies, waits for them, and re-layouts: 238 us -> 276 us
    unnamed x46 -> x108, local copies, waits for them, and re-layouts: 22.3 us -> 59.3 us
where the time goes in v1:
time: 848 us; the launch traced here: 842 us
  local copies, waits for them, and re-layouts  276 us (33%)
  other arithmetic  254 us (30%)
  waiting for transfers between devices  174 us (21%)
  starting transfers between devices  127 us (15%)
    ppermute x32, waiting for transfers between devices, passed_along(): lax.ppermute(value, axis, [(source, source + steps) for source in range(i...  169 us
    dynamic_slice x48, local copies, waits for them, and re-layouts, plane_of(): return lax.dynamic_index_in_dim(array, index, axis, keepdims=False)  129 us
    reduce_sum x96, other arithmetic, apply_block(): return jnp.sum(block_inv * vector[None], axis=1)  116 us
    ppermute x32, starting transfers between devices, passed_along(): lax.ppermute(value, axis, [(source, source + steps) for source in range(i...  111 us
    unnamed x108, local copies, waits for them, and re-layouts  59.3 us
    dynamic_update_slice x32, local copies, waits for them, and re-layouts, step(): return (face, lax.dynamic_update_index_in_dim(sweep_output, face, index, 1))  54.3 us
    reduce_sum x32, other arithmetic, multiply_maps(): return jnp.sum(left[:, :, None, :] * right[None], axis=1)  21.3 us
    add x16, other arithmetic, step(): plane_of(driving_term, index, 1) + plane_of(decay, index, 1) * face  17.3 us
  transfers between devices with their start and end apart: 38, of which 33 were waited for; matrix products, arithmetic and copies ran while one was open for 3% of the time, Pallas kernels for 0%

profile of v1, /device:TPU:3, one launch (start us, length us, event | category | flops | bytes accessed | tf_op | source)
XLA Modules:
  0.0 841.6 jit_solution(70006610215615546)
XLA Ops:
  23.7 6.5 all-to-all-start
  34.3 11.0 %copy.51 = f32[5,5,8,8192]{3,1,0,2:T(8,128)} copy(f32[5,5,8,8192]{3,2,1,0:T(8,128)} %param.38) | data formatting | bytes 13107200
  62.3 36.2 %while.178 = (s32[]{:T(128)}, f32[5,5,8192]{2,1,0:T(8,128)S(1)}, f32[5,8192]{1,0:T(8,128)}, f32[5,5,8,8192]{3,1,0,2:T(8,128)}, f32[5,8,8192]{2,0,1:T(8,128)S(1)}, /*index=5*/f32[5,8,8192]{2,0,1:T(8,128)}, s32[]{:T(128)}) while((s32[]{:T(128)}, f32[5,5,8192]{2,1,0:T(8,128)S(1)}, f32[5,8192]{1,0:T(8,128)}, f32[5,5,8,8192]{3,1,0,2:T(8,128)}, ...), condition=%wide.region_4.5_spmd, body=%wide.region_1.4_spmd.sunk | while | flops 2498562 | bytes 7209049 | solution.py:57
  101.2 79.5 %while.179 = (s32[]{:T(128)}, f32[5,8192]{1,0:T(8,128)}, f32[5,8192]{1,0:T(8,128)}, f32[5,5,8192]{2,1,0:T(8,128)S(1)}, f32[5,8192]{1,0:T(8,128)}, /*index=5*/s32[]{:T(128)}) while((s32[]{:T(128)}, f32[5,8192]{1,0:T(8,128)}, f32[5,8192]{1,0:T(8,128)}, f32[5,5,8192]{2,1,0:T(8,128)S(1)}, f32[5,8192]{1,0:T(8,128)}, /*index=5*/s32[]{:T(128)}) %tuple.342), condition=%wide.region_7.8_spmd, body=%wide.region_5.7_spmd.sunk | while | flops 409602 | bytes 3604645 | solution.py:179
  101.2 4.0 collective-permute-start
  110.0 5.3 collective-permute-start
  120.1 5.3 collective-permute-start
  130.2 5.3 collective-permute-start
  140.3 5.3 collective-permute-start
  150.4 5.3 collective-permute-start
  160.5 5.3 collective-permute-start
  170.6 5.3 collective-permute-start
  181.6 54.0 %while.180 = (s32[]{:T(128)}, f32[5,8192]{1,0:T(8,128)S(1)}, f32[5,8,8192]{2,1,0:T(8,128)S(1)}, f32[5,5,8,8192]{3,2,1,0:T(8,128)}, f32[5,8,8192]{2,0,1:T(8,128)}...) while((s32[]{:T(128)}, f32[5,8192]{1,0:T(8,128)S(1)}, f32[5,8,8192]{2,1,0:T(8,128)S(1)}, ...), condition=%wide.region_10.11_spmd, body=%wide.region_8.10_spmd.sunk | while | flops 450562 | bytes 4096097 | solution.py:88
  182.7 3.6 constant_dynamic-slice_fusion.16
  189.5 3.6 constant_dynamic-slice_fusion.16
  196.2 3.6 constant_dynamic-slice_fusion.16
  203.0 3.6 constant_dynamic-slice_fusion.16
  209.7 3.6 constant_dynamic-slice_fusion.16
  216.5 3.6 constant_dynamic-slice_fusion.16
  223.2 3.6 constant_dynamic-slice_fusion.16
  230.0 3.6 constant_dynamic-slice_fusion.16
  236.6 31.9 %while.188 = (s32[]{:T(128)}, f32[5,5,8192]{2,1,0:T(8,128)S(1)}, f32[5,8192]{1,0:T(8,128)S(1)}, f32[5,5,8,8192]{3,1,0,2:T(8,128)}, f32[5,8,8192]{2,0,1:T(8,128)}...) while((s32[]{:T(128)}, f32[5,5,8192]{2,1,0:T(8,128)S(1)}, ...), condition=%wide.region_14.15_spmd.clone, body=%wide.region_11.14_spmd.clone.sunk | while | flops 2539527 | bytes 7700649 | solution.py:74
  269.9 80.3 %while.181 = (s32[]{:T(128)}, f32[5,8192]{1,0:T(8,128)}, f32[5,8192]{1,0:T(8,128)}, f32[5,5,8192]{2,1,0:T(8,128)S(1)}, f32[5,8192]{1,0:T(8,128)S(1)}, /*index=5*/s32[]{:T(128)}) while((s32[]{:T(128)}, f32[5,8192]{1,0:T(8,128)}, f32[5,8192]{1,0:T(8,128)}, f32[5,5,8192]{2,1,0:T(8,128)S(1)}, f32[5,8192]{1,0:T(8,128)S(1)}, ...), condition=%wide.region_17.18_spmd, body=%wide.region_15.17_spmd.sunk | while | flops 409602 | bytes 2949257 | solution.py:188
  271.8 7.5 collective-permute-done.1
  282.4 6.9 collective-permute-done.1
  292.4 6.9 collective-permute-done.1
  302.3 6.9 collective-permute-done.1
  312.3 6.9 collective-permute-done.1
  322.2 6.9 collective-permute-done.1
  332.2 6.9 collective-permute-done.1
  342.1 6.9 collective-permute-done.1
  351.3 82.2 %while.182 = (s32[]{:T(128)}, f32[5,8192]{1,0:T(8,128)S(1)}, f32[5,8,8192]{2,1,0:T(8,128)}, f32[5,8,8192]{2,1,0:T(8,128)S(1)}, f32[5,5,8,8192]{3,2,1,0:T(8,128)}...) while((s32[]{:T(128)}, f32[5,8192]{1,0:T(8,128)S(1)}, ...), condition=%wide.region_20.21_spmd, body=%wide.region_18.20_spmd.sunk | while | flops 491526 | bytes 4751523 | solution.py:102
  351.3 3.7 constant_dynamic-slice_fusion.17
  357.4 4.2 dynamic_update_slice.41
  367.6 4.2 dynamic_update_slice.41
  377.9 4.2 dynamic_update_slice.41
  388.1 4.2 dynamic_update_slice.41
  398.4 4.2 dynamic_update_slice.41
  408.7 4.2 dynamic_update_slice.41
  418.9 4.2 dynamic_update_slice.41
  429.2 4.2 dynamic_update_slice.41
  462.7 4.8 all-to-all-done.1
  475.7 38.1 %while.183 = (s32[]{:T(128)}, f32[5,5,8192]{2,1,0:T(8,128)S(1)}, f32[5,8192]{1,0:T(8,128)S(1)}, f32[5,5,8,8192]{3,1,0,2:T(8,128)}, f32[5,8,8192]{2,0,1:T(8,128)}, /*index=5*/f32[5,8,8192]{2,0,1:T(8,128)}, s32[]{:T(128)}) while((s32[]{:T(128)}, f32[5,5,8192]{2,1,0:T(8,128)S(1)}, f32[5,8192]{1,0:T(8,128)S(1)}, f32[5,5,8,8192]{3,1,0,2:T(8,128)}, ...), condition=%wide.region_24.25_spmd, body=%wide.region_21.24_spmd.sunk | while | flops 2498562 | bytes 7209049 | solution.py:57
  515.2 78.0 %while.184 = (s32[]{:T(128)}, f32[5,8192]{1,0:T(8,128)}, f32[5,8192]{1,0:T(8,128)}, f32[5,5,8192]{2,1,0:T(8,128)S(1)}, f32[5,8192]{1,0:T(8,128)S(1)}, /*index=5*/s32[]{:T(128)}) while((s32[]{:T(128)}, f32[5,8192]{1,0:T(8,128)}, f32[5,8192]{1,0:T(8,128)}, f32[5,5,8192]{2,1,0:T(8,128)S(1)}, f32[5,8192]{1,0:T(8,128)S(1)}, ...), condition=%wide.region_27.28_spmd, body=%wide.region_25.27_spmd.sunk | while | flops 409602 | bytes 2949257 | solution.py:179
  523.5 5.2 collective-permute-start.2
  533.5 5.2 collective-permute-start.2
  543.4 5.2 collective-permute-start.2
  553.4 5.2 collective-permute-start.2
  563.4 5.2 collective-permute-start.2
  573.3 5.2 collective-permute-start.2
  583.3 5.2 collective-permute-start.2
  594.2 54.0 %while.185 = (s32[]{:T(128)}, f32[5,8192]{1,0:T(8,128)S(1)}, f32[5,8,8192]{2,1,0:T(8,128)S(1)}, f32[5,5,8,8192]{3,2,1,0:T(8,128)}, f32[5,8,8192]{2,0,1:T(8,128)}...) while((s32[]{:T(128)}, f32[5,8192]{1,0:T(8,128)S(1)}, f32[5,8,8192]{2,1,0:T(8,128)S(1)}, ...), condition=%wide.region_30.31_spmd, body=%wide.region_28.30_spmd.sunk | while | flops 450562 | bytes 4096097 | solution.py:88
  595.3 3.6 constant_dynamic-slice_fusion.18
  649.4 42.2 %while.189 = (s32[]{:T(128)}, f32[5,5,8192]{2,1,0:T(8,128)S(1)}, f32[5,8192]{1,0:T(8,128)S(1)}, f32[5,5,8,8192]{3,1,0,2:T(8,128)}, f32[5,8,8192]{2,0,1:T(8,128)}...) while((s32[]{:T(128)}, f32[5,5,8192]{2,1,0:T(8,128)S(1)}, ...), condition=%wide.region_34.35_spmd.clone, body=%wide.region_31.34_spmd.clone.sunk | while | flops 2539527 | bytes 7700649 | solution.py:74
  693.0 80.3 %while.186 = (s32[]{:T(128)}, f32[5,8192]{1,0:T(8,128)}, f32[5,8192]{1,0:T(8,128)}, f32[5,5,8192]{2,1,0:T(8,128)S(1)}, f32[5,8192]{1,0:T(8,128)S(1)}, /*index=5*/s32[]{:T(128)}) while((s32[]{:T(128)}, f32[5,8192]{1,0:T(8,128)}, f32[5,8192]{1,0:T(8,128)}, f32[5,5,8192]{2,1,0:T(8,128)S(1)}, f32[5,8192]{1,0:T(8,128)S(1)}, ...), condition=%wide.region_37.38_spmd, body=%wide.region_35.37_spmd.sunk | while | flops 409602 | bytes 2949257 | solution.py:188
  694.9 7.5 collective-permute-done.3
  705.5 6.9 collective-permute-done.3
  715.5 6.9 collective-permute-done.3
  725.4 6.9 collective-permute-done.3
  735.4 6.9 collective-permute-done.3
  745.4 6.9 collective-permute-done.3
  755.3 6.9 collective-permute-done.3
  765.3 6.9 collective-permute-done.3
  774.3 65.9 %while.187 = (s32[]{:T(128)}, f32[5,8192]{1,0:T(8,128)S(1)}, f32[5,8,8192]{2,1,0:T(8,128)S(1)}, f32[5,8,8192]{2,1,0:T(8,128)}, f32[5,5,8,8192]{3,2,1,0:T(8,128)}...) while((s32[]{:T(128)}, f32[5,8192]{1,0:T(8,128)S(1)}, ...), condition=%wide.region_40.41_spmd, body=%wide.region_38.40_spmd.sunk | while | flops 491526 | bytes 4751523 | solution.py:102
  (643 shorter events, 556.3 us)
Async XLA Ops:
  0.6 1.5 copy-start.23
  0.6 1.7 copy-start.21
  3.0 1.2 copy-start.20
  3.0 27.2 %copy-start.11 = (f32[5,8,8192]{2,1,0:T(8,128)S(1)}, f32[5,8,8192]{2,1,0:T(8,128)}, u32[]{:S(2)}) copy-start(f32[5,8,8192]{2,1,0:T(8,128)} %param.36) | copy-start | bytes 3932164
  3.0 30.5 %copy-start.19 = (s32[8,8192]{1,0:T(8,128)S(1)}, s32[8,8192]{1,0:T(8,128)}, u32[]{:S(2)}) copy-start(s32[8,8192]{1,0:T(8,128)} %param.42) | copy-start | bytes 786436
  23.7 25.0 %all-to-all-start = ((f32[32,5,2,128]{3,2,1,0:T(2,128)}), f32[32,5,2,128]{3,2,1,0:T(2,128)}, u32[]{:S(2)}, u32[]{:S(2)}) async-start(f32[32,5,2,128]{3,2,1,0:T(2,128)} %constant_dynamic-update-slice_fusion), calls=%async_computation | async-start | bytes 327680 | tf_op jit(solution)/shard_map/all_to_all | solution.py:160
  30.3 26.5 %collective-permute-start.4 = (f32[5,8,1]{2,1,0:T(8,128)S(1)}, f32[5,8,1]{2,1,0:T(8,128)S(1)}, u32[]{:S(2)}, u32[]{:S(2)}) collective-permute-start(f32[5,8,1]{2,1,0:T(8,128)S(1)} %get-tuple-element.1522), channel_id=1, source_target_pairs={{0,1},{1,2},{2,3},{3,0},{4,5},{5,6},{6,7},{7,4},{8,9},{9,10},{10,1... | collective-permute-start | bytes 488 | tf_op jit(solution)/shard_map/ppermute | solution.py:17
  31.5 25.3 %collective-permute-start.5 = (f32[5,8,1]{2,1,0:T(8,128)S(1)}, f32[5,8,1]{2,1,0:T(8,128)S(1)}, u32[]{:S(2)}, u32[]{:S(2)}) collective-permute-start(f32[5,8,1]{2,1,0:T(8,128)S(1)} %get-tuple-element.1523), channel_id=1, source_target_pairs={{1,0},{2,1},{3,2},{0,3},{5,4},{6,5},{7,6},{4,7},{9,8},{10,9},{11,1... | collective-permute-start | bytes 488 | tf_op jit(solution)/shard_map/ppermute | solution.py:19
  34.3 11.0 %copy-start.16 = (f32[5,8,8192]{2,1,0:T(8,128)S(1)}, f32[5,8,8192]{2,1,0:T(8,128)}, u32[]{:S(2)}) copy-start(f32[5,8,8192]{2,1,0:T(8,128)} %param.39) | copy-start | bytes 3932164
  45.2 1.3 copy-start.17
  46.6 3.1 copy-start.22
  98.6 2.6 copy-start.4
  101.2 8.1 copy-start.5
  101.2 7.6 collective-permute-start
  108.8 1.2 copy-start
  110.0 9.4 %copy-start.5 = (f32[5,8192]{1,0:T(8,128)S(1)}, f32[5,8192]{1,0:T(8,128)}, u32[]{:S(2)}) copy-start(f32[5,8192]{1,0:T(8,128)} %get-tuple-element.2013) | copy-start | bytes 491524 | tf_op jit(solution)/shard_map/while
  110.0 8.9 %collective-permute-start = (f32[5,8192]{1,0:T(8,128)}, f32[5,8192]{1,0:T(8,128)S(1)}, u32[]{:S(2)}, u32[]{:S(2)}) collective-permute-start(f32[5,8192]{1,0:T(8,128)} %get-tuple-element.2004), channel_id=1, source_target_pairs={{0,4},{4,8},{8,12},{12,16},{16,20},{20,24},{24,28},{1,5},{5,9},{9,... | collective-permute-start | bytes 491528 | tf_op jit(solution)/shard_map/while/body/eval_jaxpr/ppermute | solution.py:29
  118.9 1.2 copy-start
  120.1 9.4 %copy-start.5 = (f32[5,8192]{1,0:T(8,128)S(1)}, f32[5,8192]{1,0:T(8,128)}, u32[]{:S(2)}) copy-start(f32[5,8192]{1,0:T(8,128)} %get-tuple-element.2013) | copy-start | bytes 491524 | tf_op jit(solution)/shard_map/while
  120.1 8.9 %collective-permute-start = (f32[5,8192]{1,0:T(8,128)}, f32[5,8192]{1,0:T(8,128)S(1)}, u32[]{:S(2)}, u32[]{:S(2)}) collective-permute-start(f32[5,8192]{1,0:T(8,128)} %get-tuple-element.2004), channel_id=1, source_target_pairs={{0,4},{4,8},{8,12},{12,16},{16,20},{20,24},{24,28},{1,5},{5,9},{9,... | collective-permute-start | bytes 491528 | tf_op jit(solution)/shard_map/while/body/eval_jaxpr/ppermute | solution.py:29
  129.0 1.2 copy-start
  130.2 9.4 %copy-start.5 = (f32[5,8192]{1,0:T(8,128)S(1)}, f32[5,8192]{1,0:T(8,128)}, u32[]{:S(2)}) copy-start(f32[5,8192]{1,0:T(8,128)} %get-tuple-element.2013) | copy-start | bytes 491524 | tf_op jit(solution)/shard_map/while
  130.2 8.9 %collective-permute-start = (f32[5,8192]{1,0:T(8,128)}, f32[5,8192]{1,0:T(8,128)S(1)}, u32[]{:S(2)}, u32[]{:S(2)}) collective-permute-start(f32[5,8192]{1,0:T(8,128)} %get-tuple-element.2004), channel_id=1, source_target_pairs={{0,4},{4,8},{8,12},{12,16},{16,20},{20,24},{24,28},{1,5},{5,9},{9,... | collective-permute-start | bytes 491528 | tf_op jit(solution)/shard_map/while/body/eval_jaxpr/ppermute | solution.py:29
  139.1 1.2 copy-start
  140.3 9.4 %copy-start.5 = (f32[5,8192]{1,0:T(8,128)S(1)}, f32[5,8192]{1,0:T(8,128)}, u32[]{:S(2)}) copy-start(f32[5,8192]{1,0:T(8,128)} %get-tuple-element.2013) | copy-start | bytes 491524 | tf_op jit(solution)/shard_map/while
  140.3 8.9 %collective-permute-start = (f32[5,8192]{1,0:T(8,128)}, f32[5,8192]{1,0:T(8,128)S(1)}, u32[]{:S(2)}, u32[]{:S(2)}) collective-permute-start(f32[5,8192]{1,0:T(8,128)} %get-tuple-element.2004), channel_id=1, source_target_pairs={{0,4},{4,8},{8,12},{12,16},{16,20},{20,24},{24,28},{1,5},{5,9},{9,... | collective-permute-start | bytes 491528 | tf_op jit(solution)/shard_map/while/body/eval_jaxpr/ppermute | solution.py:29
  149.2 1.2 copy-start
  150.4 9.4 %copy-start.5 = (f32[5,8192]{1,0:T(8,128)S(1)}, f32[5,8192]{1,0:T(8,128)}, u32[]{:S(2)}) copy-start(f32[5,8192]{1,0:T(8,128)} %get-tuple-element.2013) | copy-start | bytes 491524 | tf_op jit(solution)/shard_map/while
  150.4 8.9 %collective-permute-start = (f32[5,8192]{1,0:T(8,128)}, f32[5,8192]{1,0:T(8,128)S(1)}, u32[]{:S(2)}, u32[]{:S(2)}) collective-permute-start(f32[5,8192]{1,0:T(8,128)} %get-tuple-element.2004), channel_id=1, source_target_pairs={{0,4},{4,8},{8,12},{12,16},{16,20},{20,24},{24,28},{1,5},{5,9},{9,... | collective-permute-start | bytes 491528 | tf_op jit(solution)/shard_map/while/body/eval_jaxpr/ppermute | solution.py:29
  160.5 9.4 %copy-start.5 = (f32[5,8192]{1,0:T(8,128)S(1)}, f32[5,8192]{1,0:T(8,128)}, u32[]{:S(2)}) copy-start(f32[5,8192]{1,0:T(8,128)} %get-tuple-element.2013) | copy-start | bytes 491524 | tf_op jit(solution)/shard_map/while
  160.5 8.9 %collective-permute-start = (f32[5,8192]{1,0:T(8,128)}, f32[5,8192]{1,0:T(8,128)S(1)}, u32[]{:S(2)}, u32[]{:S(2)}) collective-permute-start(f32[5,8192]{1,0:T(8,128)} %get-tuple-element.2004), channel_id=1, source_target_pairs={{0,4},{4,8},{8,12},{12,16},{16,20},{20,24},{24,28},{1,5},{5,9},{9,... | collective-permute-start | bytes 491528 | tf_op jit(solution)/shard_map/while/body/eval_jaxpr/ppermute | solution.py:29
  170.6 9.4 %copy-start.5 = (f32[5,8192]{1,0:T(8,128)S(1)}, f32[5,8192]{1,0:T(8,128)}, u32[]{:S(2)}) copy-start(f32[5,8192]{1,0:T(8,128)} %get-tuple-element.2013) | copy-start | bytes 491524 | tf_op jit(solution)/shard_map/while
  170.6 8.9 %collective-permute-start = (f32[5,8192]{1,0:T(8,128)}, f32[5,8192]{1,0:T(8,128)S(1)}, u32[]{:S(2)}, u32[]{:S(2)}) collective-permute-start(f32[5,8192]{1,0:T(8,128)} %get-tuple-element.2004), channel_id=1, source_target_pairs={{0,4},{4,8},{8,12},{12,16},{16,20},{20,24},{24,28},{1,5},{5,9},{9,... | collective-permute-start | bytes 491528 | tf_op jit(solution)/shard_map/while/body/eval_jaxpr/ppermute | solution.py:29
  269.9 9.4 %collective-permute-start.1 = (f32[5,8192]{1,0:T(8,128)}, f32[5,8192]{1,0:T(8,128)S(1)}, u32[]{:S(2)}, u32[]{:S(2)}) collective-permute-start(f32[5,8192]{1,0:T(8,128)} %get-tuple-element.2076), channel_id=1, source_target_pairs={{4,0},{8,4},{12,8},{16,12},{20,16},{24,20},{28,24},{5,1},{9,5},{13... | collective-permute-start | bytes 491528 | tf_op jit(solution)/shard_map/while/body/eval_jaxpr/ppermute | solution.py:29
  280.5 8.8 %collective-permute-start.1 = (f32[5,8192]{1,0:T(8,128)}, f32[5,8192]{1,0:T(8,128)S(1)}, u32[]{:S(2)}, u32[]{:S(2)}) collective-permute-start(f32[5,8192]{1,0:T(8,128)} %get-tuple-element.2076), channel_id=1, source_target_pairs={{4,0},{8,4},{12,8},{16,12},{20,16},{24,20},{28,24},{5,1},{9,5},{13... | collective-permute-start | bytes 491528 | tf_op jit(solution)/shard_map/while/body/eval_jaxpr/ppermute | solution.py:29
  290.5 8.8 %collective-permute-start.1 = (f32[5,8192]{1,0:T(8,128)}, f32[5,8192]{1,0:T(8,128)S(1)}, u32[]{:S(2)}, u32[]{:S(2)}) collective-permute-start(f32[5,8192]{1,0:T(8,128)} %get-tuple-element.2076), channel_id=1, source_target_pairs={{4,0},{8,4},{12,8},{16,12},{20,16},{24,20},{28,24},{5,1},{9,5},{13... | collective-permute-start | bytes 491528 | tf_op jit(solution)/shard_map/while/body/eval_jaxpr/ppermute | solution.py:29
  300.4 8.8 %collective-permute-start.1 = (f32[5,8192]{1,0:T(8,128)}, f32[5,8192]{1,0:T(8,128)S(1)}, u32[]{:S(2)}, u32[]{:S(2)}) collective-permute-start(f32[5,8192]{1,0:T(8,128)} %get-tuple-element.2076), channel_id=1, source_target_pairs={{4,0},{8,4},{12,8},{16,12},{20,16},{24,20},{28,24},{5,1},{9,5},{13... | collective-permute-start | bytes 491528 | tf_op jit(solution)/shard_map/while/body/eval_jaxpr/ppermute | solution.py:29
  310.4 8.8 %collective-permute-start.1 = (f32[5,8192]{1,0:T(8,128)}, f32[5,8192]{1,0:T(8,128)S(1)}, u32[]{:S(2)}, u32[]{:S(2)}) collective-permute-start(f32[5,8192]{1,0:T(8,128)} %get-tuple-element.2076), channel_id=1, source_target_pairs={{4,0},{8,4},{12,8},{16,12},{20,16},{24,20},{28,24},{5,1},{9,5},{13... | collective-permute-start | bytes 491528 | tf_op jit(solution)/shard_map/while/body/eval_jaxpr/ppermute | solution.py:29
  320.3 8.8 %collective-permute-start.1 = (f32[5,8192]{1,0:T(8,128)}, f32[5,8192]{1,0:T(8,128)S(1)}, u32[]{:S(2)}, u32[]{:S(2)}) collective-permute-start(f32[5,8192]{1,0:T(8,128)} %get-tuple-element.2076), channel_id=1, source_target_pairs={{4,0},{8,4},{12,8},{16,12},{20,16},{24,20},{28,24},{5,1},{9,5},{13... | collective-permute-start | bytes 491528 | tf_op jit(solution)/shard_map/while/body/eval_jaxpr/ppermute | solution.py:29
  330.3 8.8 %collective-permute-start.1 = (f32[5,8192]{1,0:T(8,128)}, f32[5,8192]{1,0:T(8,128)S(1)}, u32[]{:S(2)}, u32[]{:S(2)}) collective-permute-start(f32[5,8192]{1,0:T(8,128)} %get-tuple-element.2076), channel_id=1, source_target_pairs={{4,0},{8,4},{12,8},{16,12},{20,16},{24,20},{28,24},{5,1},{9,5},{13... | collective-permute-start | bytes 491528 | tf_op jit(solution)/shard_map/while/body/eval_jaxpr/ppermute | solution.py:29
  340.2 8.8 %collective-permute-start.1 = (f32[5,8192]{1,0:T(8,128)}, f32[5,8192]{1,0:T(8,128)S(1)}, u32[]{:S(2)}, u32[]{:S(2)}) collective-permute-start(f32[5,8192]{1,0:T(8,128)} %get-tuple-element.2076), channel_id=1, source_target_pairs={{4,0},{8,4},{12,8},{16,12},{20,16},{24,20},{28,24},{5,1},{9,5},{13... | collective-permute-start | bytes 491528 | tf_op jit(solution)/shard_map/while/body/eval_jaxpr/ppermute | solution.py:29
  351.3 82.2 %copy-start.12 = (f32[5,8,8192]{2,1,0:T(8,128)S(1)}, f32[5,8,8192]{2,1,0:T(8,128)}, u32[]{:S(2)}) copy-start(f32[5,8,8192]{2,1,0:T(8,128)} %param.36) | copy-start | bytes 3932164
  456.4 11.0 %all-to-all-start.1 = ((f32[32,5,2,128]{3,2,1,0:T(2,128)}), f32[32,5,2,128]{3,2,1,0:T(2,128)S(1)}, u32[]{:S(2)}, u32[]{:S(2)}) async-start(f32[32,5,2,128]{3,2,1,0:T(2,128)} %constant_dynamic-update-slice_fusion.32), calls=%async_computation.1 | async-start | bytes 327680 | tf_op jit(solution)/shard_map/all_to_all | solution.py:160
  459.4 11.9 %collective-permute-start.6 = (f32[5,8,1]{2,1,0:T(8,128)S(1)}, f32[5,8,1]{2,1,0:T(8,128)S(1)}, u32[]{:S(2)}, u32[]{:S(2)}) collective-permute-start(f32[5,8,1]{2,1,0:T(8,128)S(1)} %get-tuple-element.1520), channel_id=1, source_target_pairs={{0,1},{1,2},{2,3},{3,0},{4,5},{5,6},{6,7},{7,4},{8,9},{9,10},{10,1... | collective-permute-start | bytes 488 | tf_op jit(solution)/shard_map/ppermute | solution.py:17
  460.6 10.8 %collective-permute-start.7 = (f32[5,8,1]{2,1,0:T(8,128)S(1)}, f32[5,8,1]{2,1,0:T(8,128)S(1)}, u32[]{:S(2)}, u32[]{:S(2)}) collective-permute-start(f32[5,8,1]{2,1,0:T(8,128)S(1)} %get-tuple-element.1521), channel_id=1, source_target_pairs={{1,0},{2,1},{3,2},{0,3},{5,4},{6,5},{7,6},{4,7},{9,8},{10,9},{11,1... | collective-permute-start | bytes 488 | tf_op jit(solution)/shard_map/ppermute | solution.py:19
  469.7 1.6 copy-start.15
  469.7 1.6 copy-start.18
  515.2 7.1 collective-permute-start.2
  523.5 8.8 %collective-permute-start.2 = (f32[5,8192]{1,0:T(8,128)}, f32[5,8192]{1,0:T(8,128)S(1)}, u32[]{:S(2)}, u32[]{:S(2)}) collective-permute-start(f32[5,8192]{1,0:T(8,128)} %get-tuple-element.2145), channel_id=1, source_target_pairs={{0,4},{4,8},{8,12},{12,16},{16,20},{20,24},{24,28},{1,5},{5,9},{9,... | collective-permute-start | bytes 491528 | tf_op jit(solution)/shard_map/while/body/eval_jaxpr/ppermute | solution.py:29
  533.5 8.8 %collective-permute-start.2 = (f32[5,8192]{1,0:T(8,128)}, f32[5,8192]{1,0:T(8,128)S(1)}, u32[]{:S(2)}, u32[]{:S(2)}) collective-permute-start(f32[5,8192]{1,0:T(8,128)} %get-tuple-element.2145), channel_id=1, source_target_pairs={{0,4},{4,8},{8,12},{12,16},{16,20},{20,24},{24,28},{1,5},{5,9},{9,... | collective-permute-start | bytes 491528 | tf_op jit(solution)/shard_map/while/body/eval_jaxpr/ppermute | solution.py:29
  543.4 8.8 %collective-permute-start.2 = (f32[5,8192]{1,0:T(8,128)}, f32[5,8192]{1,0:T(8,128)S(1)}, u32[]{:S(2)}, u32[]{:S(2)}) collective-permute-start(f32[5,8192]{1,0:T(8,128)} %get-tuple-element.2145), channel_id=1, source_target_pairs={{0,4},{4,8},{8,12},{12,16},{16,20},{20,24},{24,28},{1,5},{5,9},{9,... | collective-permute-start | bytes 491528 | tf_op jit(solution)/shard_map/while/body/eval_jaxpr/ppermute | solution.py:29
  553.4 8.8 %collective-permute-start.2 = (f32[5,8192]{1,0:T(8,128)}, f32[5,8192]{1,0:T(8,128)S(1)}, u32[]{:S(2)}, u32[]{:S(2)}) collective-permute-start(f32[5,8192]{1,0:T(8,128)} %get-tuple-element.2145), channel_id=1, source_target_pairs={{0,4},{4,8},{8,12},{12,16},{16,20},{20,24},{24,28},{1,5},{5,9},{9,... | collective-permute-start | bytes 491528 | tf_op jit(solution)/shard_map/while/body/eval_jaxpr/ppermute | solution.py:29
  563.4 8.8 %collective-permute-start.2 = (f32[5,8192]{1,0:T(8,128)}, f32[5,8192]{1,0:T(8,128)S(1)}, u32[]{:S(2)}, u32[]{:S(2)}) collective-permute-start(f32[5,8192]{1,0:T(8,128)} %get-tuple-element.2145), channel_id=1, source_target_pairs={{0,4},{4,8},{8,12},{12,16},{16,20},{20,24},{24,28},{1,5},{5,9},{9,... | collective-permute-start | bytes 491528 | tf_op jit(solution)/shard_map/while/body/eval_jaxpr/ppermute | solution.py:29
  573.3 8.8 %collective-permute-start.2 = (f32[5,8192]{1,0:T(8,128)}, f32[5,8192]{1,0:T(8,128)S(1)}, u32[]{:S(2)}, u32[]{:S(2)}) collective-permute-start(f32[5,8192]{1,0:T(8,128)} %get-tuple-element.2145), channel_id=1, source_target_pairs={{0,4},{4,8},{8,12},{12,16},{16,20},{20,24},{24,28},{1,5},{5,9},{9,... | collective-permute-start | bytes 491528 | tf_op jit(solution)/shard_map/while/body/eval_jaxpr/ppermute | solution.py:29
  583.3 8.8 %collective-permute-start.2 = (f32[5,8192]{1,0:T(8,128)}, f32[5,8192]{1,0:T(8,128)S(1)}, u32[]{:S(2)}, u32[]{:S(2)}) collective-permute-start(f32[5,8192]{1,0:T(8,128)} %get-tuple-element.2145), channel_id=1, source_target_pairs={{0,4},{4,8},{8,12},{12,16},{16,20},{20,24},{24,28},{1,5},{5,9},{9,... | collective-permute-start | bytes 491528 | tf_op jit(solution)/shard_map/while/body/eval_jaxpr/ppermute | solution.py:29
  693.0 9.4 %collective-permute-start.3 = (f32[5,8192]{1,0:T(8,128)}, f32[5,8192]{1,0:T(8,128)S(1)}, u32[]{:S(2)}, u32[]{:S(2)}) collective-permute-start(f32[5,8192]{1,0:T(8,128)} %get-tuple-element.2217), channel_id=1, source_target_pairs={{4,0},{8,4},{12,8},{16,12},{20,16},{24,20},{28,24},{5,1},{9,5},{13... | collective-permute-start | bytes 491528 | tf_op jit(solution)/shard_map/while/body/eval_jaxpr/ppermute | solution.py:29
  703.6 8.8 %collective-permute-start.3 = (f32[5,8192]{1,0:T(8,128)}, f32[5,8192]{1,0:T(8,128)S(1)}, u32[]{:S(2)}, u32[]{:S(2)}) collective-permute-start(f32[5,8192]{1,0:T(8,128)} %get-tuple-element.2217), channel_id=1, source_target_pairs={{4,0},{8,4},{12,8},{16,12},{20,16},{24,20},{28,24},{5,1},{9,5},{13... | collective-permute-start | bytes 491528 | tf_op jit(solution)/shard_map/while/body/eval_jaxpr/ppermute | solution.py:29
  713.6 8.8 %collective-permute-start.3 = (f32[5,8192]{1,0:T(8,128)}, f32[5,8192]{1,0:T(8,128)S(1)}, u32[]{:S(2)}, u32[]{:S(2)}) collective-permute-start(f32[5,8192]{1,0:T(8,128)} %get-tuple-element.2217), channel_id=1, source_target_pairs={{4,0},{8,4},{12,8},{16,12},{20,16},{24,20},{28,24},{5,1},{9,5},{13... | collective-permute-start | bytes 491528 | tf_op jit(solution)/shard_map/while/body/eval_jaxpr/ppermute | solution.py:29
  723.5 8.8 %collective-permute-start.3 = (f32[5,8192]{1,0:T(8,128)}, f32[5,8192]{1,0:T(8,128)S(1)}, u32[]{:S(2)}, u32[]{:S(2)}) collective-permute-start(f32[5,8192]{1,0:T(8,128)} %get-tuple-element.2217), channel_id=1, source_target_pairs={{4,0},{8,4},{12,8},{16,12},{20,16},{24,20},{28,24},{5,1},{9,5},{13... | collective-permute-start | bytes 491528 | tf_op jit(solution)/shard_map/while/body/eval_jaxpr/ppermute | solution.py:29
  733.5 8.8 %collective-permute-start.3 = (f32[5,8192]{1,0:T(8,128)}, f32[5,8192]{1,0:T(8,128)S(1)}, u32[]{:S(2)}, u32[]{:S(2)}) collective-permute-start(f32[5,8192]{1,0:T(8,128)} %get-tuple-element.2217), channel_id=1, source_target_pairs={{4,0},{8,4},{12,8},{16,12},{20,16},{24,20},{28,24},{5,1},{9,5},{13... | collective-permute-start | bytes 491528 | tf_op jit(solution)/shard_map/while/body/eval_jaxpr/ppermute | solution.py:29
  743.4 8.8 %collective-permute-start.3 = (f32[5,8192]{1,0:T(8,128)}, f32[5,8192]{1,0:T(8,128)S(1)}, u32[]{:S(2)}, u32[]{:S(2)}) collective-permute-start(f32[5,8192]{1,0:T(8,128)} %get-tuple-element.2217), channel_id=1, source_target_pairs={{4,0},{8,4},{12,8},{16,12},{20,16},{24,20},{28,24},{5,1},{9,5},{13... | collective-permute-start | bytes 491528 | tf_op jit(solution)/shard_map/while/body/eval_jaxpr/ppermute | solution.py:29
  753.4 8.8 %collective-permute-start.3 = (f32[5,8192]{1,0:T(8,128)}, f32[5,8192]{1,0:T(8,128)S(1)}, u32[]{:S(2)}, u32[]{:S(2)}) collective-permute-start(f32[5,8192]{1,0:T(8,128)} %get-tuple-element.2217), channel_id=1, source_target_pairs={{4,0},{8,4},{12,8},{16,12},{20,16},{24,20},{28,24},{5,1},{9,5},{13... | collective-permute-start | bytes 491528 | tf_op jit(solution)/shard_map/while/body/eval_jaxpr/ppermute | solution.py:29
  763.3 8.8 %collective-permute-start.3 = (f32[5,8192]{1,0:T(8,128)}, f32[5,8192]{1,0:T(8,128)S(1)}, u32[]{:S(2)}, u32[]{:S(2)}) collective-permute-start(f32[5,8192]{1,0:T(8,128)} %get-tuple-element.2217), channel_id=1, source_target_pairs={{4,0},{8,4},{12,8},{16,12},{20,16},{24,20},{28,24},{5,1},{9,5},{13... | collective-permute-start | bytes 491528 | tf_op jit(solution)/shard_map/while/body/eval_jaxpr/ppermute | solution.py:29
  840.1 1.5 copy-start.14
  (34 other events, 38.4 us)
